TPU v7x, 128 devices: a whole 4x4x4 slice. The times are simulated.
128 devices in a mesh: op: 8 (over y, core), tm: 16 (over z, x).
Axes of the slice: x: 4, y: 4, z: 4, core: 2. Of those that a mesh axis runs over, the one named last changes fastest.
Arguments:
- mesons: float32 [8, 32, 2, 384, 384], P('op', 'tm'), may hold values from -6 to 6
- perambulator: float32 [32, 2, 384, 384], P('tm', None, 'op'), may hold values from -0.21875 to 0.21875
- graph_list: int32 [64, 4], P('op'), may hold values from -2 to 7, as said below
Outputs:
- diagrams: float32 [384, 6144], P('op', 'tm')
Inputs may be any that keep to these rules, and one draw needn't show every extreme that they name: `graph_list`: each row is a product slot of the op index that holds it: first operator id and second operator id (0 to 7, the second taken at the sink time), diagram id (0 to 7) and an integer weight. Weight 0 marks an empty slot; live weights are -2, -1, 1 or 2 and the live slots of an op index come first. In every draw some op index has all 8 slots live.
All inputs are finite; a program needn't handle non-finite values.
Results may differ from a plain program's by a relative error of at most 0.0003.
Values sent between devices are 32-bit elements; how exact they have to be, the bound alone decides.
A program may use at most 128 MiB of HBM per device.

v0:
```python
import jax
import jax.numpy as jnp
from jax import lax
from jax.sharding import PartitionSpec as P

N = 384
DIAG = 8


HIGHEST = lax.Precision.HIGHEST


def shifted(array, axis, by):
    size = lax.axis_size(axis)
    return lax.ppermute(array, axis, [(i, (i + by) % size) for i in range(size)])


def matmul_high(first, second):
    return jnp.matmul(first, second, precision=HIGHEST)


def complex_product(first, second):
    first_real = first[..., 0, :, :]
    first_imag = first[..., 1, :, :]
    second_real = second[..., 0, :, :]
    second_imag = second[..., 1, :, :]
    real_part = matmul_high(first_real, second_real) - matmul_high(first_imag, second_imag)
    imag_part = matmul_high(first_real, second_imag) + matmul_high(first_imag, second_real)
    return jnp.stack([real_part, imag_part], axis=-3)


def adjoint(matrix):
    swapped = jnp.swapaxes(matrix, -1, -2)
    return jnp.stack([swapped[..., 0, :, :], -swapped[..., 1, :, :]], axis=-3)


def contract(entries, current, sink_side, factor):
    row_count = current.shape[3]
    width = sink_side.shape[4]

    def accumulate(slot, totals):
        entry = entries[slot]

        def include(totals):
            first_factor = lax.dynamic_index_in_dim(current, entry[0], 0, keepdims=False)
            second_factor = lax.dynamic_index_in_dim(sink_side, entry[1], 0, keepdims=False)
            product = jnp.sum(complex_product(first_factor, second_factor), axis=0)
            product = jnp.swapaxes(product, 0, 1)
            previous = lax.dynamic_index_in_dim(totals, entry[2], 1, keepdims=False)
            updated = previous + entry[3].astype(jnp.float32) * factor * product
            return lax.dynamic_update_index_in_dim(totals, updated, entry[2], 1)

        return lax.cond(entry[3] != 0, include, lambda unchanged: unchanged, totals)

    totals = lax.fori_loop(
        0, entries.shape[0], accumulate, jnp.zeros((row_count, DIAG, 2, width), jnp.float32)
    )
    return totals.reshape(row_count, DIAG * 2 * width)


def local(mesons, perambulator, graph_list):
    local_times = mesons.shape[1]
    full_tau = lax.all_gather(perambulator, "op", axis=2, tiled=True)
    dressed = complex_product(adjoint(full_tau)[None], complex_product(mesons, full_tau[None]))
    factor = (2.0 * N) ** (-0.5) / (local_times * lax.axis_size("tm"))
    current = lax.all_gather(dressed, "op", axis=0, tiled=True)
    sink_side = shifted(current, "tm", -1)
    flattened = contract(graph_list, current, sink_side, factor)
    partial_rows = lax.psum_scatter(flattened, "op", scatter_dimension=0, tiled=True)
    return lax.psum_scatter(partial_rows, "tm", scatter_dimension=1, tiled=True)


def solution(mesh):
    placed = (P("op", "tm", None, None, None), P("tm", None, "op", None), P("op", None))
    return jax.shard_map(
        local, mesh=mesh, in_specs=placed, out_specs=P("op", "tm"), check_vma=False
    )
```

profile of v0, /device:TPU:0, one launch (start us, length us, event | category | flops | bytes accessed | tf_op | source)
XLA Modules:
  0.0 941.0 jit_solution(16170886792856757249)
XLA Ops:
  8.3 28.9 %all-gather.3.cloned.1.call-done = f32[2,2,384,384]{3,2,0,1:T(8,128)} async-done(((f32[2,2,48,384]{3,2,0,1:T(8,128)}), f32[2,2,384,384]{3,2,0,1:T(8,128)}) %all-gather.3.cloned.1.call-update) | async-done | bytes 2359312 | tf_op jit(solution)/shard_map/all_gather | solution.py:63
  37.2 4.2 fusion.10
  41.4 3.9 fusion.8
  45.3 2.4 convolution_subtract_fusion.2
  47.9 2.4 convolution_add_fusion.2
  50.5 3.0 fusion.13
  53.6 2.5 fusion.12
  56.1 2.5 fusion.5
  58.6 2.5 fusion.4
  63.0 94.4 %all-gather.5.cloned.1.call-done = f32[8,2,2,384,384]{4,3,2,1,0:T(8,128)} async-done(((f32[1,2,2,384,384]{4,3,2,1,0:T(8,128)}), f32[8,2,2,384,384]{4,3,2,1,0:T(8,128)}) %all-gather.5.cloned.1.call-update) | async-done | bytes 18874384 | tf_op jit(solution)/shard_map/all_gather | solution.py:66
  157.4 5.2 collective-permute-start
  162.7 12.6 %copy.21 = f32[8,2,2,384,384]{4,3,1,2,0:T(8,128)} copy(f32[8,2,2,384,384]{4,3,2,1,0:T(8,128)} %all-gather.5.cloned.1.call-done) | data formatting | bytes 37748736 | tf_op jit(solution)/shard_map/while | solution.py:55
  175.3 392.5 %collective-permute-done = f32[8,2,2,384,384]{4,3,2,1,0:T(8,128)} collective-permute-done((f32[8,2,2,384,384]{4,3,2,1,0:T(8,128)}, f32[8,2,2,384,384]{4,3,2,1,0:T(8,128)}, u32[]{:S(2)}, u32[]{:S(2)}) %collective-permute-start) | collective-permute-done | bytes 18874400 | tf_op jit(solution)/shard_map/ppermute | solution.py:15
  567.8 12.6 %copy.22 = f32[8,2,2,384,384]{4,3,1,2,0:T(8,128)} copy(f32[8,2,2,384,384]{4,3,2,1,0:T(8,128)} %collective-permute-done) | data formatting | bytes 37748736 | tf_op jit(solution)/shard_map/while | solution.py:55
  580.4 4.6 broadcast_in_dim.9
  585.0 32.7 %while.16 = (s32[]{:T(128)}, f32[384,8,2,384]{3,0,2,1:T(8,128)}, s32[8,4]{1,0:T(8,128)S(1)}, f32[8,2,2,384,384]{4,3,1,2,0:T(8,128)}, f32[8,2,2,384,384]{4,3,1,2,0:T(8,128)}, /*index=5*/s32[]{:T(128)}, s32[1,1]{1,0:T(1,128)}) while((s32[]{:T(128)}, f32[384,8,2,384]{3,0,2,1:T(8,128)}, s32[8,4]{1,0:T(8,128)S(1)}, ...), condition=%wide.region_4.5_spmd, body=%wide.region_0.4_spmd.sunk | while | flops 5437882368 | bytes 35390296 | solution.py:55
  586.4 22.1 %conditional.2 = (f32[384,8,2,384]{3,0,2,1:T(8,128)}) conditional(s32[]{:T(128)} %bitcast.80, f32[384,8,2,384]{3,0,2,1:T(8,128)} %get-tuple-element.188, (s32[1,4]{1,0:T(1,128)S(1)}, f32[384,8,2,384]{3,0,2,1:T(8,128)}, f32[8,2,2,384,384]{4,3,1,2,0:T(8,128)}, f32[8,2,2,384,384]{4,3,1,2,0:T(8,128)}) %tuple.46), branch_computations={%region_1.0_spmd, %region_2.3_spmd} | conditional | flops 5437882368 | bytes 35390128 | solution.py:53
  590.8 2.7 dynamic-slice_bitcast_fusion
  595.9 2.4 fusion.1
  600.8 2.4 fusion
  617.8 17.5 %copy.23 = f32[384,8,2,384]{3,2,1,0:T(2,128)} copy(f32[384,8,2,384]{3,0,2,1:T(8,128)} %get-tuple-element.120) | data formatting | bytes 18874368 | tf_op jit(solution)/shard_map/while | solution.py:55
  635.3 12.4 %reshape.28 = f32[384,6144]{1,0:T(8,128)} reshape(f32[384,8,2,384]{3,2,1,0:T(2,128)} %copy.23) | data formatting | bytes 18874368 | tf_op jit(solution)/shard_map/reshape | solution.py:58
  647.8 210.9 %reduce-scatter.3.cloned.1.call-done = f32[48,6144]{1,0:T(8,128)} async-done(((f32[384,6144]{1,0:T(8,128)}), f32[48,6144]{1,0:T(8,128)}) %reduce-scatter.3.cloned.1.call-update) | async-done | bytes 1179664 | tf_op jit(solution)/shard_map/reduce_scatter | solution.py:69
  858.7 75.6 %reduce-scatter.5.cloned.1.call-done = f32[48,384]{1,0:T(8,128)} async-done(((f32[48,6144]{1,0:T(8,128)}), f32[48,384]{1,0:T(8,128)}) %reduce-scatter.5.cloned.1.call-update) | async-done | bytes 73744 | tf_op jit(solution)/shard_map/reduce_scatter | solution.py:70
  (49 shorter events, 17.5 us)
Async XLA Ops:
  6.5 30.6 %all-gather.3.cloned.1.call-start = ((), (), s32[]{:S(2)}) async-start(), calls=%async_computation.2 | async-start | bytes 2654208 | tf_op jit(solution)/shard_map/all_gather | solution.py:63
  8.3 149.2 %all-gather.5.cloned.1.call-start = ((), (), s32[]{:S(2)}) async-start(), calls=%async_computation.3 | async-start | bytes 21233664 | tf_op jit(solution)/shard_map/all_gather | solution.py:66
  37.2 4.2 copy-start
  41.4 3.9 copy-start.1
  62.9 99.7 %copy-start.2 = (s32[8,4]{0,1:T(4,128)S(1)}, s32[8,4]{0,1:T(4,128)}, u32[]{:S(2)}) copy-start(s32[8,4]{0,1:T(4,128)} %param.9) | copy-start | bytes 388
  62.9 795.7 %reduce-scatter.3.cloned.1.call-start = ((), (), s32[]{:S(2)}) async-start(), calls=%async_computation.4 | async-start | bytes 10616832 | tf_op jit(solution)/shard_map/reduce_scatter | solution.py:69
  157.4 410.4 %collective-permute-start = (f32[8,2,2,384,384]{4,3,2,1,0:T(8,128)}, f32[8,2,2,384,384]{4,3,2,1,0:T(8,128)}, u32[]{:S(2)}, u32[]{:S(2)}) collective-permute-start(f32[8,2,2,384,384]{4,3,2,1,0:T(8,128)} %all-gather.5.cloned.1.call-done), channel_id=1, source_target_pairs={{0,15},{1,0},{2,1},{3,2},{4,3},{5,4},{6,5},{7,6},{8,7},{9,8},{10,9... | collective-permute-start | bytes 56623112 | tf_op jit(solution)/shard_map/ppermute | solution.py:15
  647.7 286.5 %reduce-scatter.5.cloned.1.call-start = ((), (), s32[]{:S(2)}) async-start(), calls=%async_computation.5 | async-start | bytes 1253376 | tf_op jit(solution)/shard_map/reduce_scatter | solution.py:70
Sparse Core Ops, SparseCore 0:
  9.0 28.0 all-gather.2
  63.1 94.3 all-gather.4
  647.8 210.7 reduce-scatter.2
  861.7 72.4 reduce-scatter.4
where the time goes:
time: 951 us; the launch traced here: 941 us
  waiting for transfers between devices  802 us (84%)
  local copies, waits for them, and re-layouts  73.1 us (8%)
  matrix products  33.3 us (4%)
  between operations  13.5 us (1%)
  loops' own time  11.7 us (1%)
    ppermute x1, waiting for transfers between devices, shifted(): lax.ppermute(array, axis, [(i, (i + by) % size) for i in range(size)])  392 us
    reduce_scatter x1, waiting for transfers between devices, local(): lax.psum_scatter(flattened, 'op', scatter_dimension=0, tiled=True)  211 us
    all_gather x1, waiting for transfers between devices, local(): current = lax.all_gather(dressed, 'op', axis=0, tiled=True)  94.4 us
    reduce_scatter x1, waiting for transfers between devices, local(): return lax.psum_scatter(partial_rows, 'tm', scatter_dimension=1, tiled=True)  75.6 us
    while x4, local copies, waits for them, and re-layouts, contract(): lax.fori_loop(0, entries.shape[0], accumulate, jnp.zeros((row_count, DIAG...  42.8 us
    dot_general x12, matrix products, matmul_high(): return jnp.matmul(first, second, precision=HIGHEST)  33.3 us
    all_gather x1, waiting for transfers between devices, local(): full_tau = lax.all_gather(perambulator, 'op', axis=2, tiled=True)  28.9 us
  transfers between devices with their start and end apart: 5, of which 5 were waited for; matrix products, arithmetic and copies ran while one was open for 1% of the time, Pallas kernels for 0%

commit v1 on v0

v1 whole, which is shorter than its diff:
```python
import functools

import jax
import jax.numpy as jnp
from jax import lax
from jax.experimental import pallas as pl
from jax.experimental.pallas import tpu as pltpu
from jax.sharding import PartitionSpec as P

N = 384
DIAG = 8
OPS = 8
BLK = N // 8
CH = 128
NCH = N // CH
HALF = CH // 2
SUB = HALF // 4
F32 = jnp.float32
BF16 = jnp.bfloat16
MESH = pl.DeviceIdType.MESH
RELS = [(dy, dc) for dy in (1, 3, 2, 0) for dc in (0, 1)]


def halves(value):
    high = value.astype(BF16)
    return high, (value - high.astype(F32)).astype(BF16)


def dot3(a_high, a_low, b_high, b_low):
    dot = functools.partial(jnp.dot, preferred_element_type=F32)
    return dot(a_high, b_high) + (dot(a_high, b_low) + dot(a_low, b_high))


def rows(index, size):
    return pl.ds(pl.multiple_of(index * size, size), size)


def kernel(
    mesons, tau, table, out,
    wall, wsum, wsm, taus, lhs1, lhs2, rhs, dres, drest, abuf, bbuf, ehi, elo,
    lmain, prod, cbuf, s1x, s1z, r0, r1, s2x, s2z, sbuf, fin,
    w_s, w_r, w_l, t_s, t_r, f_s, f_r, a_s, a_r, b_s, b_r, c_s, c_r,
    x1_s, x1_r, z1_s, z1_r, x2_s, x2_r, z2_s, z2_r, y_s, y_r,
):
    op, tm = lax.axis_index("op"), lax.axis_index("tm")
    y, c, z, x = op // 2, op % 2, tm // 4, tm % 4

    def device(dy=0, dc=0, dz=0, dx=0):
        return (((y + dy) % 4) * 2 + (c + dc) % 2, ((z + dz) % 4) * 4 + (x + dx) % 4)

    def column(dy, dc, dj):
        return (((y + dy) % 4) * 2 + (c + dc) % 2, (tm + dj + 16) % 16)

    def source(dy, dc):
        return ((y - dy + 4) % 4) * 2 + (c + dc) % 2

    def remote(src, dst, send, recv, where):
        return pltpu.make_async_remote_copy(
            src_ref=src, dst_ref=dst, send_sem=send, recv_sem=recv, device_id=where, device_id_type=MESH
        )

    greet = [column(dy, dc, dj) for dj in (0, 1, -1) for dy, dc in RELS if (dy, dc, dj) != (0, 0, 0)]
    greet += [device(dx=k) for k in (1, 2, 3)] + [device(dz=k) for k in (1, 2, 3)]
    barrier = pltpu.get_barrier_semaphore()
    for where in greet:
        pl.semaphore_signal(barrier, inc=1, device_id=where, device_id_type=MESH)
    pl.semaphore_wait(barrier, len(greet))

    waits = []

    near = [(k, dy, dc) for k, (dy, dc) in enumerate(RELS) if (dy, dc) != (0, 0)]

    def tau_copy(t, dy):
        dc = 1 if dy == 0 else 0
        return remote(
            tau.at[t], taus.at[t, :, rows(op, BLK), :], t_s.at[t, dy], t_r.at[t, dy], device(dy=dy, dc=dc)
        )

    def tau_forward(t, dy):
        block = taus.at[t, :, rows(source(dy, 0), BLK), :]
        return remote(block, block, f_s.at[t, dy], f_r.at[t, dy], device(dc=1))

    def table_copy(k, dy, dc):
        return remote(table, wall.at[op], w_s.at[k], w_r.at[k], device(dy=dy, dc=dc))

    for dy in (1, 3, 2, 0):
        tau_copy(0, dy).start()
    for dy in (1, 3, 2, 0):
        tau_copy(1, dy).start()
    for k, dy, dc in near:
        table_copy(k, dy, dc).start()
    wall[op] = table[...]
    for t in range(2):
        taus[t, :, rows(op, BLK), :] = tau[t]
        for p in range(2):
            high, low = halves(mesons[0, t, p])
            lhs1[t, 0, :, p * N : (p + 1) * N] = high
            lhs1[t, 1, :, p * N : (p + 1) * N] = low
    for k, dy, dc in near:
        table_copy(k, dy, dc).wait()
    total = wall[0]
    for k in range(1, 8):
        total = total + wall[k]
    wsum[...] = total
    to_scalars = pltpu.make_async_copy(wsum, wsm, w_l)
    to_scalars.start()

    def set_rhs(top_real, top_imag, low_real, low_imag):
        for r, (left, right) in enumerate(((top_real, top_imag), (low_real, low_imag))):
            for q, value in enumerate((left, right)):
                high, low = halves(value)
                rhs[0, r * N : (r + 1) * N, q * N : (q + 1) * N] = high
                rhs[1, r * N : (r + 1) * N, q * N : (q + 1) * N] = low

    def dress(t):
        for dy in (1, 3, 2):
            tau_copy(t, dy).wait_recv()
            tau_forward(t, dy).start()
        tau_copy(t, 0).wait_recv()
        for dy in (1, 3, 2):
            tau_forward(t, dy).wait_recv()
        real, imag = taus[t, 0], taus[t, 1]
        set_rhs(real, imag, -imag, real)
        for p in range(2):
            high, low = halves(jnp.transpose(taus[t, p]))
            lhs2[0, :, p * N : (p + 1) * N] = high
            lhs2[1, :, p * N : (p + 1) * N] = low
        half = dot3(lhs1[t, 0], lhs1[t, 1], rhs[0], rhs[1])
        real, imag = half[:, :N], half[:, N:]
        set_rhs(real, imag, imag, -real)
        full = dot3(lhs2[0], lhs2[1], rhs[0], rhs[1])
        dres[t, 0] = full[:, :N]
        dres[t, 1] = full[:, N:]

    def turn(t):
        for p in range(2):
            for m in range(NCH):
                picked = jnp.concatenate(
                    [
                        dres[t, p, BLK * (2 * yy + cc) + SUB * m : BLK * (2 * yy + cc) + SUB * (m + 1), :]
                        for cc in range(2)
                        for yy in range(4)
                    ],
                    axis=0,
                )
                drest[t, p, :, CH * m : CH * (m + 1)] = jnp.transpose(picked)

    def b_copy(t, k, dy, dc):
        where = column(dy, dc, -1 if t == 0 else 0)
        return remote(
            dres.at[t, :, rows(where[0], BLK), :],
            bbuf.at[:, pl.ds(pl.multiple_of(t * N + op * BLK, 16), BLK), :],
            b_s.at[t, k], b_r.at[t, k], where,
        )

    def a_copy(t, m, k, dy, dc):
        where = column(dy, dc, 1 if t == 1 else 0)
        lanes = pl.ds(m * CH, CH)
        return remote(
            drest.at[t, :, rows(where[0], BLK), lanes],
            abuf.at[:, pl.ds(pl.multiple_of(t * N + op * BLK, 16), BLK), lanes],
            a_s.at[t, m, k], a_r.at[t, m, k], where,
        )

    def b_rels(t):
        return [(k, dy, dc) for k, (dy, dc) in enumerate(RELS) if t == 0 or (dy, dc) != (0, 0)]

    def a_rels(t):
        return [(k, dy, dc) for k, (dy, dc) in enumerate(RELS) if t == 1 or (dy, dc) != (0, 0)]

    dress(0)
    for k, dy, dc in b_rels(0):
        b_copy(0, k, dy, dc).start()
    turn(0)
    dress(1)
    for k, dy, dc in b_rels(1):
        b_copy(1, k, dy, dc).start()
    turn(1)
    for m in range(NCH):
        for t in range(2):
            for k, dy, dc in a_rels(t):
                a_copy(t, m, k, dy, dc).start()
    mine = rows(op, BLK)
    abuf[:, mine, :] = drest[0, :, mine, :]
    bbuf[:, pl.ds(pl.multiple_of(N + op * BLK, 16), BLK), :] = dres[1, :, mine, :]

    to_scalars.wait()

    def weigh(t):
        def body(n, carry):
            d, a = n // OPS, n % OPS
            for p in range(2):
                total = None
                for b in range(OPS):
                    weight = wsm[n // 16, (n % 16) * 8 + b]
                    term = weight * bbuf[p, t * N + b * BLK : t * N + (b + 1) * BLK, :]
                    total = term if total is None else total + term
                high, low = halves(total)
                where = pl.ds(pl.multiple_of(t * N + a * BLK, 16), BLK)
                ehi[d, where, p * N : (p + 1) * N] = high
                elo[d, where, p * N : (p + 1) * N] = low
            return carry

        lax.fori_loop(0, DIAG * OPS, body, 0)

    for t in range(2):
        for k, dy, dc in b_rels(t):
            b_copy(t, k, dy, dc).wait_recv()
        weigh(t)

    own = rows(c, HALF)
    other = rows(1 - c, HALF)

    def core_copy(m, d):
        zz, xx = d // 2, (d % 2) * 2
        return remote(
            prod.at[m, zz, pl.ds(xx, 2), other, :], cbuf.at[m, zz, pl.ds(xx, 2)],
            c_s.at[m, d], c_r.at[m, d], device(dc=1),
        )

    def main(m):
        for t in range(2):
            for k, dy, dc in a_rels(t):
                a_copy(t, m, k, dy, dc).wait_recv()
        for p in range(2):
            high, low = halves(jnp.transpose(abuf[p, :, m * CH : (m + 1) * CH]))
            lmain[0, p * CH : (p + 1) * CH, :] = high
            lmain[1, p * CH : (p + 1) * CH, :] = low

        def body(d, carry):
            both = dot3(lmain[0], lmain[1], ehi[d], elo[d])
            zz, xx = d // 2, (d % 2) * 2
            prod[m, zz, xx] = both[:CH, :N] - both[CH:, N:]
            prod[m, zz, xx + 1] = both[:CH, N:] + both[CH:, :N]
            core_copy(m, d).start()
            return carry

        lax.fori_loop(0, DIAG, body, 0)

    top = pl.ds(pl.multiple_of(c * HALF, HALF), HALF // 2)
    low_half = pl.ds(pl.multiple_of(c * HALF + HALF // 2, HALF // 2), HALF // 2)

    def x1_copy(m, k):
        return remote(
            prod.at[m, :, (x + k) % 4, top, :], s1x.at[m, k - 1], x1_s.at[m, k - 1], x1_r.at[m, k - 1], device(dx=k)
        )

    def z1_copy(m, k):
        return remote(
            prod.at[m, (z + k) % 4, :, low_half, :], s1z.at[m, k - 1], z1_s.at[m, k - 1], z1_r.at[m, k - 1], device(dz=k)
        )

    def z2_copy(m, k):
        return remote(r0.at[m, (z + k) % 4], s2z.at[m, k - 1], z2_s.at[m, k - 1], z2_r.at[m, k - 1], device(dz=k))

    def x2_copy(m, k):
        return remote(r1.at[m, (x + k) % 4], s2x.at[m, k - 1], x2_s.at[m, k - 1], x2_r.at[m, k - 1], device(dx=k))

    def y_copy(m, k):
        return remote(
            sbuf.at[m, rows((y + k) % 4, SUB), :], fin.at[m, k - 1], y_s.at[m, k - 1], y_r.at[m, k - 1], device(dy=k)
        )

    def stage0(m):
        def body(d, carry):
            core_copy(m, d).wait_recv()
            zz, xx = d // 2, (d % 2) * 2
            for p in range(2):
                prod[m, zz, xx + p, own, :] = prod[m, zz, xx + p, own, :] + cbuf[m, zz, xx + p]
            return carry

        lax.fori_loop(0, DIAG, body, 0)
        for k in (1, 3, 2):
            x1_copy(m, k).start()
            z1_copy(m, k).start()

    def stage1(m):
        for k in (1, 3, 2):
            x1_copy(m, k).wait_recv()
            z1_copy(m, k).wait_recv()
        for q in range(4):
            r0[m, q] = (prod[m, q, x, top, :] + s1x[m, 0, q]) + (s1x[m, 1, q] + s1x[m, 2, q])
            r1[m, q] = (prod[m, z, q, low_half, :] + s1z[m, 0, q]) + (s1z[m, 1, q] + s1z[m, 2, q])
        for k in (1, 3, 2):
            z2_copy(m, k).start()
            x2_copy(m, k).start()

    def stage2(m):
        for k in (1, 3, 2):
            z2_copy(m, k).wait_recv()
            x2_copy(m, k).wait_recv()
        sbuf[m, : HALF // 2] = (r0[m, z] + s2z[m, 0]) + (s2z[m, 1] + s2z[m, 2])
        sbuf[m, HALF // 2 :] = (r1[m, x] + s2x[m, 0]) + (s2x[m, 1] + s2x[m, 2])
        for k in (1, 3, 2):
            y_copy(m, k).start()

    def stage3(m):
        for k in (1, 3, 2):
            y_copy(m, k).wait_recv()
        out[m * SUB : (m + 1) * SUB, :] = (sbuf[m, rows(y, SUB), :] + fin[m, 0]) + (fin[m, 1] + fin[m, 2])

    main(0)
    stage0(0)
    main(1)
    stage0(1)
    stage1(0)
    main(2)
    stage0(2)
    stage1(1)
    stage2(0)
    stage1(2)
    stage2(1)
    stage3(0)
    stage2(2)
    stage3(1)
    stage3(2)

    for t in range(2):
        for dy in (1, 3, 2, 0):
            tau_copy(t, dy).wait_send()
        for dy in (1, 3, 2):
            tau_forward(t, dy).wait_send()
        for k, dy, dc in b_rels(t):
            b_copy(t, k, dy, dc).wait_send()
        for m in range(NCH):
            for k, dy, dc in a_rels(t):
                a_copy(t, m, k, dy, dc).wait_send()
    for m in range(NCH):
        for d in range(DIAG):
            core_copy(m, d).wait_send()
        for k in (1, 2, 3):
            for copy in (x1_copy, z1_copy, x2_copy, z2_copy, y_copy):
                copy(m, k).wait_send()


def local(mesons, perambulator, graph_list):
    times = mesons.shape[1] * lax.axis_size("tm")
    factor = (2.0 * N) ** (-0.5) / times
    place = (graph_list[:, 2] * OPS + graph_list[:, 0]) * OPS + graph_list[:, 1]
    weight = graph_list[:, 3].astype(F32) * factor
    table = jnp.sum(
        jnp.where(place[:, None, None] == jnp.arange(1024, dtype=jnp.int32).reshape(8, 128), weight[:, None, None], 0.0),
        axis=0,
    )
    dma = pltpu.SemaphoreType.DMA
    vmem = pltpu.VMEM
    q = HALF // 2
    return pl.pallas_call(
        kernel,
        out_shape=jax.ShapeDtypeStruct((BLK, N), F32),
        in_specs=[pl.BlockSpec(memory_space=pltpu.VMEM)] * 3,
        out_specs=pl.BlockSpec(memory_space=pltpu.VMEM),
        scratch_shapes=[
            vmem((8, 8, 128), F32), vmem((8, 128), F32), pltpu.SMEM((8, 128), F32),
            vmem((2, 2, N, N), F32),
            vmem((2, 2, N, 2 * N), BF16), vmem((2, N, 2 * N), BF16), vmem((2, 2 * N, 2 * N), BF16),
            vmem((2, 2, N, N), F32), vmem((2, 2, N, N), F32),
            vmem((2, 2 * N, N), F32), vmem((2, 2 * N, N), F32),
            vmem((DIAG, 2 * N, 2 * N), BF16), vmem((DIAG, 2 * N, 2 * N), BF16),
            vmem((2, 2 * CH, 2 * N), BF16),
            vmem((NCH, 4, 4, CH, N), F32), vmem((NCH, 4, 4, HALF, N), F32),
            vmem((NCH, 3, 4, q, N), F32), vmem((NCH, 3, 4, q, N), F32),
            vmem((NCH, 4, q, N), F32), vmem((NCH, 4, q, N), F32),
            vmem((NCH, 3, q, N), F32), vmem((NCH, 3, q, N), F32),
            vmem((NCH, HALF, N), F32), vmem((NCH, 3, SUB, N), F32),
            dma((8,)), dma((8,)), dma,
            dma((2, 4)), dma((2, 4)), dma((2, 4)), dma((2, 4)),
            dma((2, NCH, 8)), dma((2, NCH, 8)), dma((2, 8)), dma((2, 8)),
            dma((NCH, 8)), dma((NCH, 8)),
        ] + [dma((NCH, 3))] * 10,
        compiler_params=pltpu.CompilerParams(
            collective_id=0, has_side_effects=True, vmem_limit_bytes=64 * 2**20 - 2**19
        ),
    )(mesons, perambulator, table)


def solution(mesh):
    placed = (P("op", "tm", None, None, None), P("tm", None, "op", None), P("op", None))
    return jax.shard_map(
        local, mesh=mesh, in_specs=placed, out_specs=P("op", "tm"), check_vma=False
    )
```

time: 951 us -> 145 us (0.15); the launches traced: 941 us -> 145 us
  waiting for transfers between devices: 802 us -> 0 us
  Pallas kernels: 0 us -> 141 us
  local copies, waits for them, and re-layouts: 73.1 us -> 1.52 us
  matrix products: 33.3 us -> 0 us
  between operations: 13.5 us -> 0.01 us
  loops' own time: 11.7 us -> 0 us
    ppermute x1 -> x0, waiting for transfers between devices: 392 us -> none  [shifted(): lax.ppermute(array, axis, [(i, (i + by) % size) for i in range(size)])]
    reduce_scatter x2 -> x0, waiting for transfers between devices: 286 us -> none  [the longest x1 211 us: local(): lax.psum_scatter(flattened, 'op', scatter_dimension=0, tiled=True)]
    pallas_call x0 -> x1, Pallas kernels: none -> 141 us  [local(): pl.pallas_call(kernel, out_shape=jax.ShapeDtypeStruct((BLK, N), F32), in_...]
    all_gather x2 -> x0, waiting for transfers between devices: 123 us -> none  [the longest x1 94.4 us: local(): current = lax.all_gather(dressed, 'op', axis=0, tiled=True)]
    while x4 -> x0, local copies, waits for them, and re-layouts: 42.8 us -> none  [contract(): lax.fori_loop(0, entries.shape[0], accumulate, jnp.zeros((row_count, DIAG...]
    dot_general x12 -> x0, matrix products: 33.3 us -> none  [matmul_high(): return jnp.matmul(first, second, precision=HIGHEST)]
    reshape x1 -> x0, local copies, waits for them, and re-layouts: 12.4 us -> none  [contract(): return totals.reshape(row_count, DIAG * 2 * width)]
    another operation x9 -> x0, loops' own time: 11.7 us -> none  [the longest x8 6.36 us: accumulate(): return lax.cond(entry[3] != 0, include, lambda unchanged: unchanged, totals)]
  transfers between devices with their start and end apart: 5 -> 0, of which waited for: 5 -> 0; matrix products, arithmetic and copies ran while one was open for 1% -> 0% of each run, Pallas kernels for 0% -> 0%
where the time goes in v1:
time: 145 us
  Pallas kernels  141 us (97%)
  other arithmetic  2.17 us (1%)
  local copies, waits for them, and re-layouts  1.52 us (1%)
    pallas_call x1, Pallas kernels, local(): pl.pallas_call(kernel, out_shape=jax.ShapeDtypeStruct((BLK, N), F32), in_...  141 us

profile of v1, /device:TPU:0, one launch (start us, length us, event | category | flops | bytes accessed | tf_op | source)
XLA Modules:
  0.0 145.2 jit_solution(16755674287076852679)
XLA Ops:
  0.0 0.7 multiply_bitcast_fusion
  0.7 0.8 add_bitcast_fusion
  1.5 0.7 select_reduce_fusion.table
  2.2 141.5 %shard_map.37 = f32[48,384]{1,0:T(8,128)} custom-call(f32[1,2,2,384,384]{4,3,2,1,0:T(8,128)} %mesons.1, f32[2,2,48,384]{3,2,1,0:T(8,128)} %tau.1, f32[8,128]{1,0:T(8,128)} %select_reduce_fusion.table), custom_call_target="tpu_custom_call" | custom-call | tf_op jit(solution)/shard_map/pallas_call | solution.py:348
  143.7 1.5 %copy.5 = f32[48,384]{1,0:T(8,128)} copy(f32[48,384]{1,0:T(8,128)} %shard_map.37) | data formatting | bytes 147456
  (1 shorter events, 0.0 us)

commit v2 on v1

v2 whole, which is shorter than its diff:
```python
import functools

import jax
import jax.numpy as jnp
from jax import lax
from jax.experimental import pallas as pl
from jax.experimental.pallas import tpu as pltpu
from jax.sharding import PartitionSpec as P

N = 384
DIAG = 8
OPS = 8
BLK = N // 8
CH = 128
NCH = N // CH
HALF = CH // 2
SUB = HALF // 4
F32 = jnp.float32
BF16 = jnp.bfloat16
MESH = pl.DeviceIdType.MESH
RELS = [(dy, dc) for dy in (1, 3, 2, 0) for dc in (0, 1)]


def halves(value):
    high = value.astype(BF16)
    return high, (value - high.astype(F32)).astype(BF16)


def dot3(a_high, a_low, b_high, b_low):
    dot = functools.partial(jnp.dot, preferred_element_type=F32)
    return dot(a_high, b_high) + (dot(a_high, b_low) + dot(a_low, b_high))


def rows(index, size):
    return pl.ds(pl.multiple_of(index * size, size), size)


def kernel(
    mesons_hbm, tau, graph, out,
    mesons, table, wall, wide, kron, taus, lhs1, lhs2, rhs, dres, drest, abuf, bbuf, ehi, elo,
    prod, cbuf, s1, r1, s2, r2, s3,
    m_l, w_s, w_r, t_s, t_r, f_s, f_r, a_s, a_r, b_s, b_r, c_s, c_r,
    s1_s, s1_r, s2_s, s2_r, s3_s, s3_r,
):
    op, tm = lax.axis_index("op"), lax.axis_index("tm")
    y, c, z, x = op // 2, op % 2, tm // 4, tm % 4

    def device(dy=0, dc=0, dz=0, dx=0):
        return (((y + dy) % 4) * 2 + (c + dc) % 2, ((z + dz) % 4) * 4 + (x + dx) % 4)

    def column(dy, dc, dj):
        return (((y + dy) % 4) * 2 + (c + dc) % 2, (tm + dj + 16) % 16)

    def source(dy, dc):
        return ((y - dy + 4) % 4) * 2 + (c + dc) % 2

    def remote(src, dst, send, recv, where):
        return pltpu.make_async_remote_copy(
            src_ref=src, dst_ref=dst, send_sem=send, recv_sem=recv, device_id=where, device_id_type=MESH
        )

    sent = []

    def send(copy):
        copy.start()
        sent.append(copy)

    greet = [column(dy, dc, dj) for dj in (0, 1, -1) for dy, dc in RELS if (dy, dc, dj) != (0, 0, 0)]
    greet += [device(dx=k) for k in (1, 2, 3)] + [device(dz=k) for k in (1, 2, 3)]
    barrier = pltpu.get_barrier_semaphore()
    for where in greet:
        pl.semaphore_signal(barrier, inc=1, device_id=where, device_id_type=MESH)
    load = pltpu.make_async_copy(mesons_hbm.at[0], mesons, m_l)
    load.start()
    table[...] = jnp.zeros_like(table)
    table[:, 0:4] = graph[...]
    pl.semaphore_wait(barrier, len(greet))

    near = [(k, dy, dc) for k, (dy, dc) in enumerate(RELS) if (dy, dc) != (0, 0)]

    def tau_copy(t, dy):
        if dy == 2:
            via = 3 if t else 1
            block = taus.at[t, :, rows(source(via, 0), BLK), :]
            return remote(block, block, t_s.at[t, dy], t_r.at[t, dy], device(dy=via))
        dc = 1 if dy == 0 else 0
        return remote(
            tau.at[t], taus.at[t, :, rows(op, BLK), :], t_s.at[t, dy], t_r.at[t, dy], device(dy=dy, dc=dc)
        )

    def tau_forward(t, dy):
        block = taus.at[t, :, rows(source(dy, 0), BLK), :]
        return remote(block, block, f_s.at[t, dy], f_r.at[t, dy], device(dc=1))

    def table_copy(k, dy, dc):
        return remote(table, wall.at[op], w_s.at[k], w_r.at[k], device(dy=dy, dc=dc))

    for t, order in ((0, (1, 3, 0)), (1, (3, 1, 0))):
        for dy in order:
            send(tau_copy(t, dy))
    for k, dy, dc in near:
        send(table_copy(k, dy, dc))
    wall[op] = table[...]
    load.wait()
    for t in range(2):
        taus[t, :, rows(op, BLK), :] = tau[t]
        for p in range(2):
            high, low = halves(mesons[t, p])
            lhs1[t, 0, :, p * N : (p + 1) * N] = high
            lhs1[t, 1, :, p * N : (p + 1) * N] = low
    def set_rhs(top_real, top_imag, low_real, low_imag):
        for r, (left, right) in enumerate(((top_real, top_imag), (low_real, low_imag))):
            for q, value in enumerate((left, right)):
                high, low = halves(value)
                rhs[0, r * N : (r + 1) * N, q * N : (q + 1) * N] = high
                rhs[1, r * N : (r + 1) * N, q * N : (q + 1) * N] = low

    def pass_on(t, dy):
        tau_copy(t, dy).wait_recv()
        if dy == (3 if t else 1):
            send(tau_copy(t, 2))
        send(tau_forward(t, dy))

    def dress(t):
        tau_copy(t, 0).wait_recv()
        for dy in (1, 3, 2):
            tau_forward(t, dy).wait_recv()
        real, imag = taus[t, 0], taus[t, 1]
        set_rhs(real, imag, -imag, real)
        for p in range(2):
            high, low = halves(jnp.transpose(taus[t, p]))
            lhs2[0, :, p * N : (p + 1) * N] = high
            lhs2[1, :, p * N : (p + 1) * N] = low
        half = dot3(lhs1[t, 0], lhs1[t, 1], rhs[0], rhs[1])
        real, imag = half[:, :N], half[:, N:]
        set_rhs(real, imag, imag, -real)
        full = dot3(lhs2[0], lhs2[1], rhs[0], rhs[1])
        dres[t, 0] = full[:, :N]
        dres[t, 1] = full[:, N:]

    def turn(t):
        for p in range(2):
            for m in range(NCH):
                picked = jnp.concatenate(
                    [
                        dres[t, p, BLK * (2 * yy + cc) + SUB * m : BLK * (2 * yy + cc) + SUB * (m + 1), :]
                        for cc in range(2)
                        for yy in range(4)
                    ],
                    axis=0,
                )
                drest[t, p, :, CH * m : CH * (m + 1)] = jnp.transpose(picked)

    def b_copy(t, k, dy, dc):
        where = column(dy, dc, -1 if t == 0 else 0)
        return remote(
            dres.at[t, :, rows(where[0], BLK), :],
            bbuf.at[:, pl.ds(pl.multiple_of(t * N + op * BLK, 16), BLK), :],
            b_s.at[t, k], b_r.at[t, k], where,
        )

    def a_copy(t, m, k, dy, dc):
        where = column(dy, dc, 1 if t == 1 else 0)
        lanes = pl.ds(m * CH, CH)
        return remote(
            drest.at[t, :, rows(where[0], BLK), lanes],
            abuf.at[:, pl.ds(pl.multiple_of(t * N + op * BLK, 16), BLK), lanes],
            a_s.at[t, m, k], a_r.at[t, m, k], where,
        )

    def b_rels(t):
        return [(k, dy, dc) for k, (dy, dc) in enumerate(RELS) if t == 0 or (dy, dc) != (0, 0)]

    def a_rels(t):
        return [(k, dy, dc) for k, (dy, dc) in enumerate(RELS) if t == 1 or (dy, dc) != (0, 0)]

    def send_a(m):
        for t in range(2):
            for k, dy, dc in a_rels(t):
                send(a_copy(t, m, k, dy, dc))

    for t, dy in ((0, 1), (0, 3), (1, 3), (0, 2)):
        pass_on(t, dy)
    dress(0)
    for dy in (1, 2):
        pass_on(1, dy)
    for k, dy, dc in b_rels(0):
        send(b_copy(0, k, dy, dc))
    dress(1)
    for k, dy, dc in b_rels(1):
        send(b_copy(1, k, dy, dc))
    turn(0)
    turn(1)
    send_a(0)
    mine = rows(op, BLK)
    abuf[:, mine, :] = drest[0, :, mine, :]
    bbuf[:, pl.ds(pl.multiple_of(N + op * BLK, 16), BLK), :] = dres[1, :, mine, :]
    for k, dy, dc in near:
        table_copy(k, dy, dc).wait_recv()
    slots = wall[...].reshape(64, 128)
    left = lax.broadcasted_iota(jnp.int32, (64, 128), 1) == slots[:, 2:3] * OPS + slots[:, 0:1]
    left = jnp.transpose(jnp.where(left, slots[:, 3:4].astype(F32), 0.0))
    right = lax.broadcasted_iota(jnp.int32, (64, N), 1) // BLK == slots[:, 1:2]
    wide[...] = jnp.dot(
        left[: DIAG * OPS].astype(BF16), right.astype(F32).astype(BF16), preferred_element_type=F32
    )
    same = lax.broadcasted_iota(jnp.int32, (BLK, N), 0) == lax.broadcasted_iota(jnp.int32, (BLK, N), 1) % BLK

    def widen(d, carry):
        for a in range(OPS):
            block = jnp.where(same, wide[pl.ds(d * OPS + a, 1), :], 0.0).astype(BF16)
            kron[d, a * BLK : (a + 1) * BLK, :N] = block
            kron[d, a * BLK : (a + 1) * BLK, N:] = block
        return carry

    lax.fori_loop(0, DIAG, widen, 0)

    xcat, lmain = rhs.at[0], lhs2.at[:, : 2 * CH, :]

    def weigh(t):
        for p in range(2):
            high, low = halves(bbuf[p, t * N : (t + 1) * N, :])
            xcat[:N, p * N : (p + 1) * N] = high
            xcat[N:, p * N : (p + 1) * N] = low

        def body(d, carry):
            high, low = halves(jnp.dot(kron[d], xcat[...], preferred_element_type=F32))
            ehi[d, t * N : (t + 1) * N, :] = high
            elo[d, t * N : (t + 1) * N, :] = low
            return carry

        lax.fori_loop(0, DIAG, body, 0)

    for t in range(2):
        for k, dy, dc in b_rels(t):
            b_copy(t, k, dy, dc).wait_recv()
        weigh(t)
        send_a(t + 1)

    own, other = pl.ds(c * 4, 4), pl.ds((1 - c) * 4, 4)

    def core_copy(m, d):
        zz, xx = d // 2, (d % 2) * 2
        return remote(
            prod.at[m, zz, pl.ds(xx, 2), other], cbuf.at[m, zz, pl.ds(xx, 2)],
            c_s.at[m, d], c_r.at[m, d], device(dc=1),
        )

    def main(m):
        for t in range(2):
            for k, dy, dc in a_rels(t):
                a_copy(t, m, k, dy, dc).wait_recv()
        for p in range(2):
            high, low = halves(jnp.transpose(abuf[p, :, m * CH : (m + 1) * CH]))
            lmain[0, p * CH : (p + 1) * CH, :] = high
            lmain[1, p * CH : (p + 1) * CH, :] = low

        def body(d, carry):
            both = dot3(lmain[0], lmain[1], ehi[d], elo[d])
            zz, xx = d // 2, (d % 2) * 2
            prod[m, zz, xx] = (both[:CH, :N] - both[CH:, N:]).reshape(8, SUB, N)
            prod[m, zz, xx + 1] = (both[:CH, N:] + both[CH:, :N]).reshape(8, SUB, N)
            core_copy(m, d).start()
            return carry

        lax.fori_loop(0, DIAG, body, 0)

    def hop(axis, k):
        return device(**{"d" + axis: k})

    def first_part(m, p, k):
        lanes = pl.ds(CH * p, CH)
        if p == 0:
            return prod.at[m, :, (x + k) % 4, own, :, lanes]
        if p == 1:
            return prod.at[m, (z + k) % 4, :, own, :, lanes]
        return prod.at[m, :, :, c * 4 + (y + k) % 4, :, lanes]

    def second_part(m, p, k):
        if p == 0:
            return r1.at[m, p, (z + k) % 4]
        return r1.at[m, p, :, ((y if p == 1 else x) + k) % 4]

    def third_part(m, p, k):
        return r2.at[m, p, ((y, x, z)[p] + k) % 4]

    def first_copy(m, p, k):
        return remote(
            first_part(m, p, k), s1.at[m, p, k - 1], s1_s.at[m, p, k - 1], s1_r.at[m, p, k - 1], hop("xzy"[p], k)
        )

    def second_copy(m, p, k):
        return remote(
            second_part(m, p, k), s2.at[m, p, k - 1], s2_s.at[m, p, k - 1], s2_r.at[m, p, k - 1], hop("zyx"[p], k)
        )

    def third_copy(m, p, k):
        return remote(
            third_part(m, p, k), s3.at[m, p, k - 1], s3_s.at[m, p, k - 1], s3_r.at[m, p, k - 1], hop("yxz"[p], k)
        )

    def start_all(copy, m):
        for k in (1, 3, 2):
            for p in range(3):
                send(copy(m, p, k))

    def stage0(m):
        def body(d, carry):
            core_copy(m, d).wait_recv()
            zz, xx = d // 2, (d % 2) * 2
            for p in range(2):
                prod[m, zz, xx + p, own] = prod[m, zz, xx + p, own] + cbuf[m, zz, xx + p]
            return carry

        lax.fori_loop(0, DIAG, body, 0)
        start_all(first_copy, m)

    def stage1(m):
        for p in range(3):
            for k in (1, 3, 2):
                first_copy(m, p, k).wait_recv()
            r1[m, p] = (first_part(m, p, 0)[...] + s1[m, p, 0]) + (s1[m, p, 1] + s1[m, p, 2])
            for k in (1, 3, 2):
                send(second_copy(m, p, k))

    def stage2(m):
        for p in range(3):
            for k in (1, 3, 2):
                second_copy(m, p, k).wait_recv()
            r2[m, p] = (second_part(m, p, 0)[...] + s2[m, p, 0]) + (s2[m, p, 1] + s2[m, p, 2])
            for k in (1, 3, 2):
                send(third_copy(m, p, k))

    def stage3(m):
        for p in range(3):
            for k in (1, 3, 2):
                third_copy(m, p, k).wait_recv()
            total = (third_part(m, p, 0)[...] + s3[m, p, 0]) + (s3[m, p, 1] + s3[m, p, 2])
            total = total * ((2.0 * N) ** (-0.5) / (2 * lax.axis_size("tm")))
            out[m * SUB : (m + 1) * SUB, p * CH : (p + 1) * CH] = total

    main(0)
    stage0(0)
    main(1)
    stage0(1)
    stage1(0)
    main(2)
    stage0(2)
    stage1(1)
    stage2(0)
    stage1(2)
    stage2(1)
    stage3(0)
    stage2(2)
    stage3(1)
    stage3(2)

    for copy in sent:
        copy.wait_send()
    for m in range(NCH):
        for d in range(DIAG):
            core_copy(m, d).wait_send()


def local(mesons, perambulator, graph_list):
    dma = pltpu.SemaphoreType.DMA
    vmem = pltpu.VMEM
    return pl.pallas_call(
        kernel,
        out_shape=jax.ShapeDtypeStruct((BLK, N), F32),
        in_specs=[pl.BlockSpec(memory_space=pl.ANY)] + [pl.BlockSpec(memory_space=pltpu.VMEM)] * 2,
        out_specs=pl.BlockSpec(memory_space=pltpu.VMEM),
        scratch_shapes=[
            vmem((2, 2, N, N), F32), vmem((8, 128), jnp.int32),
            vmem((8, 8, 128), jnp.int32), vmem((DIAG * OPS, N), F32), vmem((DIAG, N, 2 * N), BF16),
            vmem((2, 2, N, N), F32),
            vmem((2, 2, N, 2 * N), BF16), vmem((2, N, 2 * N), BF16), vmem((2, 2 * N, 2 * N), BF16),
            vmem((2, 2, N, N), F32), vmem((2, 2, N, N), F32),
            vmem((2, 2 * N, N), F32), vmem((2, 2 * N, N), F32),
            vmem((DIAG, 2 * N, 2 * N), BF16), vmem((DIAG, 2 * N, 2 * N), BF16),
            vmem((NCH, 4, 4, 8, SUB, N), F32), vmem((NCH, 4, 4, 4, SUB, N), F32),
            vmem((NCH, 3, 3, 4, 4, SUB, CH), F32), vmem((NCH, 3, 4, 4, SUB, CH), F32),
            vmem((NCH, 3, 3, 4, SUB, CH), F32), vmem((NCH, 3, 4, SUB, CH), F32), vmem((NCH, 3, 3, SUB, CH), F32),
            dma, dma((8,)), dma((8,)),
            dma((2, 4)), dma((2, 4)), dma((2, 4)), dma((2, 4)),
            dma((2, NCH, 8)), dma((2, NCH, 8)), dma((2, 8)), dma((2, 8)),
            dma((NCH, 8)), dma((NCH, 8)),
        ] + [dma((NCH, 3, 3))] * 6,
        compiler_params=pltpu.CompilerParams(
            collective_id=0, has_side_effects=True, vmem_limit_bytes=64 * 2**20 - 2**19
        ),
    )(mesons, perambulator, graph_list)


def solution(mesh):
    placed = (P("op", "tm", None, None, None), P("tm", None, "op", None), P("op", None))
    return jax.shard_map(
        local, mesh=mesh, in_specs=placed, out_specs=P("op", "tm"), check_vma=False
    )
```

time: 145 us -> 131 us (0.903)
  Pallas kernels: 141 us -> 128 us
  other arithmetic: 2.17 us -> 0 us
    pallas_call x1, Pallas kernels: 141 us -> 128 us  [local(): pl.pallas_call(kernel, out_shape=jax.ShapeDtypeStruct((BLK, N), F32), in_...]
where the time goes in v2:
time: 131 us
  Pallas kernels  128 us (98%)
  local copies, waits for them, and re-layouts  2.87 us (2%)
    pallas_call x1, Pallas kernels, local(): pl.pallas_call(kernel, out_shape=jax.ShapeDtypeStruct((BLK, N), F32), in_...  128 us
    unnamed x2, local copies, waits for them, and re-layouts  2.87 us

profile of v2, /device:TPU:0, one launch (start us, length us, event | category | flops | bytes accessed | tf_op | source)
XLA Modules:
  0.0 131.2 jit_solution(6229406534939351393)
XLA Ops:
  0.0 1.3 %copy.4.graph = s32[8,4]{1,0:T(8,128)} copy(s32[8,4]{0,1:T(4,128)} %param.5) | data formatting | bytes 256 | tf_op args[2]
  1.3 128.3 %shard_map.37 = f32[48,384]{1,0:T(8,128)} custom-call(f32[1,2,2,384,384]{4,3,2,1,0:T(8,128)} %mesons_hbm.1, f32[2,2,48,384]{3,2,1,0:T(8,128)} %tau.1, s32[8,4]{1,0:T(8,128)} %copy.4.graph), custom_call_target="tpu_custom_call" | custom-call | tf_op jit(solution)/shard_map/pallas_call | solution.py:368
  129.6 1.5 %copy.6 = f32[48,384]{1,0:T(8,128)} copy(f32[48,384]{1,0:T(8,128)} %shard_map.37) | data formatting | bytes 147456

commit v3 on v2

--- a/solution.py
+++ b/solution.py
@@ -18,7 +18,7 @@
 F32 = jnp.float32
 BF16 = jnp.bfloat16
 MESH = pl.DeviceIdType.MESH
-RELS = [(dy, dc) for dy in (1, 3, 2, 0) for dc in (0, 1)]
+RELS = [(1, 0), (3, 0), (2, 0), (0, 1), (3, 1), (1, 1), (2, 1), (0, 0)]
 
 
 def halves(value):

time: 131 us -> 130 us (level)
  no operation moved by 1% of the time
where the time goes in v3:
time: 130 us
  Pallas kernels  127 us (98%)
  local copies, waits for them, and re-layouts  2.87 us (2%)
    pallas_call x1, Pallas kernels, local(): pl.pallas_call(kernel, out_shape=jax.ShapeDtypeStruct((BLK, N), F32), in_...  127 us
    unnamed x2, local copies, waits for them, and re-layouts  2.87 us

profile of v3, /device:TPU:0, one launch (start us, length us, event | category | flops | bytes accessed | tf_op | source)
XLA Modules:
  0.0 129.9 jit_solution(1191223636609315837)
XLA Ops:
  0.0 1.3 %copy.4.graph = s32[8,4]{1,0:T(8,128)} copy(s32[8,4]{0,1:T(4,128)} %param.5) | data formatting | bytes 256 | tf_op args[2]
  1.3 127.0 %shard_map.37 = f32[48,384]{1,0:T(8,128)} custom-call(f32[1,2,2,384,384]{4,3,2,1,0:T(8,128)} %mesons_hbm.1, f32[2,2,48,384]{3,2,1,0:T(8,128)} %tau.1, s32[8,4]{1,0:T(8,128)} %copy.4.graph), custom_call_target="tpu_custom_call" | custom-call | tf_op jit(solution)/shard_map/pallas_call | solution.py:368
  128.4 1.5 %copy.6 = f32[48,384]{1,0:T(8,128)} copy(f32[48,384]{1,0:T(8,128)} %shard_map.37) | data formatting | bytes 147456
